TPU v7x, 32 devices: a whole 2x2x4 slice. The times are simulated.
32 devices in a mesh: ccd: 4 (over y, core), tile: 8 (over z, x).
Axes of the slice: x: 2, y: 2, z: 4, core: 2. Of those that a mesh axis runs over, the one named last changes fastest.
Arguments:
- exposures: float32 [8, 2048, 4096], P('tile', 'ccd'), may hold values from -6 to 6
- interp: bfloat16 [8, 32, 256, 128], P('tile'), may hold values from -0.375 to 0.375
- col_offsets: int32 [8, 32], P('tile'), may hold values from 0 to 30
- template: float32 [2048, 4096], P('ccd', 'tile'), may hold values from -6 to 6
- coef_table: float32 [8, 4, 3, 3], replicated, may hold values from -3 to 3
- coef_index: int32 [8, 4, 8], replicated, may hold values from 0 to 3
- intersection: int32 [8, 4, 8], replicated, may hold values 0 or 1
Outputs:
- difference: float32 [8, 2048, 4096], P('tile', 'ccd')
All inputs are finite; a program needn't handle non-finite values.
Results may differ from a plain program's by a relative error of at most 0.0029.
Values sent between devices are 32-bit elements; how exact they have to be, the bound alone decides.
A program may use at most 128 MiB of HBM per device.

v0:
```python
import jax
import jax.numpy as jnp
from jax import lax
from jax.sharding import PartitionSpec as P

HALF = 10
KSETS = 4


SIGMAS = (1.5, 3.0, 5.0)


def extended(array, sides, width):
    for axis, dim in sides:
        size, length = (lax.axis_size(axis), array.shape[dim])
        up = [(i, (i + 1) % size) for i in range(size - 1)]
        down = [(j, i) for i, j in up]
        last = lax.slice_in_dim(array, length - width, length, axis=dim)
        leading = lax.slice_in_dim(array, 0, width, axis=dim)
        before = lax.ppermute(last, axis, up)
        after = lax.ppermute(leading, axis, down)
        array = jnp.concatenate([before, array, after], axis=dim)
    return array


def basis_taps(half_width):
    positions = jnp.arange(-half_width, half_width + 1).astype(jnp.float32)
    kernels = []
    for sigma_value in SIGMAS:
        gauss = jnp.exp(-0.5 * (positions / sigma_value) ** 2)
        kernels.append(gauss / jnp.sum(gauss))
    return kernels


def smooth(padded, gauss, out_rows, out_cols):
    tap_count = gauss.shape[0]
    across = gauss[0] * padded[0:out_rows, :]
    for offset in range(1, tap_count):
        across = across + gauss[offset] * padded[offset : offset + out_rows, :]
    result = gauss[0] * across[:, 0:out_cols]
    for offset in range(1, tap_count):
        result = result + gauss[offset] * across[:, offset : offset + out_cols]
    return result


def resample(exposure_img, weights, offsets):
    row_count = exposure_img.shape[0]
    block_count = weights.shape[0]
    block_cols = weights.shape[2]
    tiles = exposure_img.astype(jnp.bfloat16).reshape(row_count, block_count, block_cols)
    first_part = jnp.take(tiles, offsets, axis=1)
    second_part = jnp.take(tiles, offsets + 1, axis=1)
    window = jnp.concatenate([first_part, second_part], axis=2)
    output = jnp.einsum("rjk,jkn->rjn", window, weights, preferred_element_type=jnp.float32)
    return output.reshape(row_count, block_count * block_cols)


def on_device(exposures, interp, col_offsets, template, coef_table, coef_index, intersection):
    row_count = exposures.shape[1]
    col_count = exposures.shape[2]
    patch_cols = template.shape[1]
    kernels = basis_taps(HALF)
    patch_row = lax.axis_index("ccd")
    my_epoch = lax.axis_index("tile")
    warped = resample(exposures[0], interp[0], col_offsets[0])
    row_coord = (jnp.arange(row_count).astype(jnp.float32) - (row_count - 1) / 2.0) / (
        row_count / 2.0
    )
    set_range = jnp.arange(KSETS)
    padded = extended(template, (("ccd", 0), ("tile", 1)), HALF)
    smoothed = [smooth(padded, gauss, row_count, patch_cols) for gauss in kernels]
    row_bases = (
        lax.all_gather(smoothed[0], "tile", axis=1, tiled=True),
        lax.all_gather(smoothed[1], "tile", axis=1, tiled=True),
        lax.all_gather(smoothed[2], "tile", axis=1, tiled=True),
    )
    set_ids = coef_index[my_epoch, patch_row]
    set_pick = (set_ids[:, None] == set_range[None, :]).astype(jnp.float32)
    kernel_coef = jnp.sum(set_pick[:, :, None, None] * coef_table[my_epoch][None], axis=1)
    column_coef = jnp.repeat(kernel_coef, patch_cols, axis=0)
    col_coord = (
        (jnp.arange(col_count) % patch_cols).astype(jnp.float32) - (patch_cols - 1) / 2.0
    ) / (patch_cols / 2.0)
    template_model = None
    for kernel_index in range(3):
        const_part = column_coef[:, kernel_index, 0][None, :]
        col_slope = column_coef[:, kernel_index, 1][None, :]
        row_slope = column_coef[:, kernel_index, 2][None, :]
        weight_map = const_part + col_slope * col_coord[None, :] + row_slope * row_coord[:, None]
        contrib = weight_map * row_bases[kernel_index]
        template_model = contrib if template_model is None else template_model + contrib
    coverage = jnp.repeat(intersection[my_epoch, patch_row].astype(jnp.float32), patch_cols)
    difference = (warped - template_model) * coverage[None, :]
    return difference[None]


def solution(mesh):
    placed = (
        P("tile", "ccd", None),
        P("tile", None, None, None),
        P("tile", None),
        P("ccd", "tile"),
        P(),
        P(),
        P(),
    )
    return jax.shard_map(
        on_device, mesh=mesh, in_specs=placed, out_specs=P("tile", "ccd", None), check_vma=False
    )
```

profile of v0, /device:TPU:1, one launch (start us, length us, event | category | flops | bytes accessed | tf_op | source)
XLA Modules:
  0.0 468.4 jit_solution(13398346818644322910)
XLA Ops:
  6.5 0.9 fusion.79
  7.5 2.1 collective-permute-start.1
  9.6 4.5 collective-permute-start
  14.1 0.6 fusion.77
  14.7 0.7 broadcast_divide_fusion
  15.3 0.7 fusion.85
  16.1 1.2 pad_maximum_fusion.3
  17.3 1.3 collective-permute-start.3
  18.6 4.0 collective-permute-start.2
  22.6 0.7 fusion.86
  23.2 3.5 collective-permute-done.3
  26.8 6.6 %collective-permute-done.2 = f32[532,10]{1,0:T(8,128)S(1)} collective-permute-done((f32[532,10]{1,0:T(8,128)S(1)}, f32[532,10]{1,0:T(8,128)S(1)}, u32[]{:S(2)}, u32[]{:S(2)}) %collective-permute-start.2) | collective-permute-done | bytes 21312 | tf_op jit(solution)/shard_map/ppermute | solution.py:20
  33.4 0.5 pad_maximum_fusion
  34.0 16.5 %multiply_add_fusion = f32[512,532]{1,0:T(8,128)S(1)} fusion(f32[532,532]{1,0:T(8,128)S(1)} %pad_maximum_fusion, f32[]{:T(128)} %bitcast.81, f32[]{:T(128)} %bitcast.80, f32[]{:T(128)} %bitcast.79, f32[]{:T(128)} %bitcast.78, f32[]{:T(128)} %bitcast.77, f32[]{:T(128)} %bitcast.76, f32[]{:T(128)} %bitcast.75, f32[]{:T(128)} %bitcast.74, f32[]{:T(128)} %bitcast.73, ...), kind=kLoop, calls=%fused_computation.11 | loop fusion | flops 11167744 | bytes 23969876 | tf_op jit(solution)/shard_map/add | solution.py:39
  50.5 19.6 %fusion.5 = f32[512,512]{1,0:T(8,128)} fusion(f32[512,532]{1,0:T(8,128)S(1)} %multiply_add_fusion, f32[]{:T(128)} %bitcast.81, f32[]{:T(128)} %bitcast.80, f32[]{:T(128)} %bitcast.79, f32[]{:T(128)} %bitcast.78, f32[]{:T(128)} %bitcast.77, f32[]{:T(128)} %bitcast.76, f32[]{:T(128)} %bitcast.75, f32[]{:T(128)} %bitcast.74, f32[]{:T(128)} %bitcast.73, ...), kind=kLoop, calls=%fused_computation.15 | loop fusion | flops 10747904 | bytes 23068756 | tf_op jit(solution)/shard_map/add | solution.py:42
  70.1 0.0 all-gather.6.cloned.1.call-start
  70.1 0.6 fusion.76
  70.7 0.7 broadcast_divide_fusion.1
  71.4 0.6 fusion.84
  72.0 0.7 fusion.83
  72.7 16.3 %multiply_add_fusion.1 = f32[512,532]{1,0:T(8,128)S(1)} fusion(f32[532,532]{1,0:T(8,128)S(1)} %pad_maximum_fusion, f32[]{:T(128)} %bitcast.57, f32[]{:T(128)} %bitcast.56, f32[]{:T(128)} %bitcast.55, f32[]{:T(128)} %bitcast.54, f32[]{:T(128)} %bitcast.53, f32[]{:T(128)} %bitcast.52, f32[]{:T(128)} %bitcast.51, f32[]{:T(128)} %bitcast.50, f32[]{:T(128)} %bitcast.49, ...), kind=kLoop, calls=%fused_computation.12 | loop fusion | flops 11167744 | bytes 23969876 | tf_op jit(solution)/shard_map/add | solution.py:39
  89.0 19.3 %fusion.25 = f32[512,512]{1,0:T(8,128)} fusion(f32[512,532]{1,0:T(8,128)S(1)} %multiply_add_fusion.1, f32[]{:T(128)} %bitcast.57, f32[]{:T(128)} %bitcast.56, f32[]{:T(128)} %bitcast.55, f32[]{:T(128)} %bitcast.54, f32[]{:T(128)} %bitcast.53, f32[]{:T(128)} %bitcast.52, f32[]{:T(128)} %bitcast.51, f32[]{:T(128)} %bitcast.50, f32[]{:T(128)} %bitcast.49, ...), kind=kLoop, calls=%fused_computation.56 | loop fusion | flops 10747904 | bytes 23068756 | tf_op jit(solution)/shard_map/add | solution.py:42
  108.3 0.2 all-gather.4.cloned.1.call-start
  108.5 0.6 fusion.75
  109.2 0.7 broadcast_divide_fusion.2
  109.8 0.7 fusion.82
  110.5 0.7 fusion.81
  111.2 16.5 %multiply_add_fusion.2 = f32[512,532]{1,0:T(8,128)S(1)} fusion(f32[532,532]{1,0:T(8,128)S(1)} %pad_maximum_fusion, f32[]{:T(128)} %bitcast.33, f32[]{:T(128)} %bitcast.32, f32[]{:T(128)} %bitcast.31, f32[]{:T(128)} %bitcast.30, f32[]{:T(128)} %bitcast.29, f32[]{:T(128)} %bitcast.28, f32[]{:T(128)} %bitcast.27, f32[]{:T(128)} %bitcast.26, f32[]{:T(128)} %bitcast.25, ...), kind=kLoop, calls=%fused_computation.13 | loop fusion | flops 11167744 | bytes 23969876 | tf_op jit(solution)/shard_map/add | solution.py:39
  127.7 19.6 %fusion.45 = f32[512,512]{1,0:T(8,128)} fusion(f32[512,532]{1,0:T(8,128)S(1)} %multiply_add_fusion.2, f32[]{:T(128)} %bitcast.33, f32[]{:T(128)} %bitcast.32, f32[]{:T(128)} %bitcast.31, f32[]{:T(128)} %bitcast.30, f32[]{:T(128)} %bitcast.29, f32[]{:T(128)} %bitcast.28, f32[]{:T(128)} %bitcast.27, f32[]{:T(128)} %bitcast.26, f32[]{:T(128)} %bitcast.25, ...), kind=kLoop, calls=%fused_computation.97 | loop fusion | flops 10747904 | bytes 23068756 | tf_op jit(solution)/shard_map/add | solution.py:42
  147.3 7.3 %copy.23 = bf16[1,512,4096]{1,2,0:T(8,128)(2,1)} copy(f32[1,512,4096]{2,1,0:T(8,128)} %param.9) | data formatting | bytes 12582912 | tf_op args[0]
  154.6 6.4 %copy.24 = bf16[512,32,128]{2,0,1:T(8,128)(2,1)} copy(bf16[512,32,128]{0,2,1:T(8,128)(2,1)} %bitcast.108) | data formatting | bytes 8388608 | tf_op jit(solution)/shard_map/convert_element_type | solution.py:50
  161.1 5.3 %gather_fusion.1 = bf16[32,512,128]{2,1,0:T(8,128)(2,1)} fusion(bf16[512,32,128]{2,0,1:T(8,128)(2,1)} %copy.24, s32[1024]{0:T(1024)S(1)} %pad_clamp_fusion), kind=kCustom, calls=%fused_computation.1.clone | custom fusion | bytes 8388736 | tf_op jit(solution)/shard_map/jit(_take)/gather | solution.py:52
  166.4 5.2 %gather_fusion = bf16[32,512,128]{2,1,0:T(8,128)(2,1)} fusion(bf16[512,32,128]{2,0,1:T(8,128)(2,1)} %copy.24, s32[1024]{0:T(1024)S(1)} %pad_clamp_fusion.1), kind=kCustom, calls=%fused_computation.clone | custom fusion | bytes 8388736 | tf_op jit(solution)/shard_map/jit(_take)/gather | solution.py:51
  171.6 5.2 %select_bitcast_fusion = (bf16[512,32,128]{2,0,1:T(8,128)(2,1)S(1)}, bf16[512,32,128]{2,0,1:T(8,128)(2,1)}) fusion(bf16[32,512,128]{2,1,0:T(8,128)(2,1)} %gather_fusion.1, pred[32]{0:T(512)(128)(4,1)S(1)} %get-tuple-element.6, bf16[32,512,128]{2,1,0:T(8,128)(2,1)} %gather_fusion, pred[32]{0:T(512)(128)(4,1)S(1)} %get-tuple-element.84), kind=kLoop, calls=%fused_computation.7 | loop fusion | flops 4194304 | bytes 16777280 | tf_op jit(solution)/shard_map/jit(_take)/select_n | solution.py:52
  176.8 8.5 %fusion = f32[32,512,128]{1,2,0:T(8,128)} fusion(bf16[512,32,128]{2,0,1:T(8,128)(2,1)S(1)} %get-tuple-element.87, bf16[512,32,128]{2,0,1:T(8,128)(2,1)} %get-tuple-element.88, bf16[1,32,256,128]{3,2,1,0:T(8,128)(2,1)S(1)} %copy-done), kind=kOutput, calls=%fused_computation.2 | convolution fusion | flops 1090519040 | bytes 18874368 | tf_op jit(solution)/shard_map/rjk,jkn->rjn/dot_general | solution.py:54
  185.3 8.9 %copy.29 = f32[512,4096]{1,0:T(8,128)} copy(f32[512,4096]{0,1:T(8,128)} %bitcast.107) | data formatting | bytes 16777216 | tf_op jit(solution)/shard_map/reshape | solution.py:55
  194.3 0.7 fusion.72
  195.0 0.1 broadcast_bitcast_fusion
  195.0 0.1 constant_dynamic-slice_fusion.1
  195.1 0.2 copy.31
  195.3 0.1 multiply_reduce_fusion
  195.4 0.1 broadcast_in_dim.15
  195.5 0.1 reshape.109
  195.6 0.1 fusion.80
  195.8 0.0 all-gather.8.cloned.1.call-done
  195.8 124.2 %all-gather.6.cloned.1.call-done = f32[512,4096]{1,0:T(8,128)} async-done(((f32[512,512]{1,0:T(8,128)}), f32[512,4096]{1,0:T(8,128)}) %all-gather.6.cloned.1.call-update) | async-done | bytes 8388624 | tf_op jit(solution)/shard_map/all_gather | solution.py:74
  319.9 125.3 %all-gather.4.cloned.1.call-done = f32[512,4096]{1,0:T(8,128)} async-done(((f32[512,512]{1,0:T(8,128)}), f32[512,4096]{1,0:T(8,128)}) %all-gather.4.cloned.1.call-update) | async-done | bytes 8388624 | tf_op jit(solution)/shard_map/all_gather | solution.py:73
  445.3 16.6 %multiply_bitcast_fusion = f32[1,512,4096]{2,1,0:T(8,128)} fusion(f32[512,4096]{1,0:T(8,128)} %copy.29, f32[512,4096]{1,0:T(8,128)} %all-gather.8.cloned.1.call-done, f32[512,4096]{1,0:T(8,128)} %all-gather.6.cloned.1.call-done, f32[512,4096]{1,0:T(8,128)} %all-gather.4.cloned.1.call-done, f32[4096]{0:T(1024)S(1)} %bitcast.112, f32[4096]{0:T(1024)S(1)} %bitcast.109, ...), kind=kLoop, calls=%fused_computation.6 | loop fusion | flops 27262976 | bytes 42059776 | tf_op jit(solution)/shard_map/broadcast_in_dim | solution.py:94
  (24 shorter events, 0.1 us)
Async XLA Ops:
  6.5 170.3 %copy-start = (bf16[1,32,256,128]{3,2,1,0:T(8,128)(2,1)S(1)}, bf16[1,32,256,128]{3,2,1,0:T(8,128)(2,1)}, u32[]{:S(2)}) copy-start(bf16[1,32,256,128]{3,2,1,0:T(8,128)(2,1)} %param.10) | copy-start | bytes 6291460
  6.5 189.2 %all-gather.8.cloned.1.call-start = ((), (), s32[]{:S(2)}) async-start(), calls=%async_computation.2 | async-start | bytes 9437184 | tf_op jit(solution)/shard_map/all_gather | solution.py:75
  6.5 26.9 %copy-start.1 = (f32[512,512]{1,0:T(8,128)S(1)}, f32[512,512]{1,0:T(8,128)}, u32[]{:S(2)}) copy-start(f32[512,512]{1,0:T(8,128)} %param.12) | copy-start | bytes 3145732
  7.5 8.6 %collective-permute-start.1 = (f32[10,512]{1,0:T(8,128)S(1)}, f32[10,512]{1,0:T(8,128)S(1)}, u32[]{:S(2)}, u32[]{:S(2)}) collective-permute-start(f32[10,512]{1,0:T(8,128)S(1)} %get-tuple-element.11), channel_id=1, source_target_pairs={{8,0},{16,8},{24,16},{9,1},{17,9},{25,17},{10,2},{18,10},{26,18},{... | collective-permute-start | bytes 61448 | tf_op jit(solution)/shard_map/ppermute | solution.py:21
  9.6 6.5 %collective-permute-start = (f32[10,512]{1,0:T(8,128)S(1)}, f32[10,512]{1,0:T(8,128)S(1)}, u32[]{:S(2)}, u32[]{:S(2)}) collective-permute-start(f32[10,512]{1,0:T(8,128)S(1)} %get-tuple-element.10), channel_id=1, source_target_pairs={{0,8},{8,16},{16,24},{1,9},{9,17},{17,25},{2,10},{10,18},{18,26},{... | collective-permute-start | bytes 61448 | tf_op jit(solution)/shard_map/ppermute | solution.py:20
  17.3 9.5 %collective-permute-start.3 = (f32[532,10]{1,0:T(8,128)S(1)}, f32[532,10]{1,0:T(8,128)S(1)}, u32[]{:S(2)}, u32[]{:S(2)}) collective-permute-start(f32[532,10]{1,0:T(8,128)S(1)} %get-tuple-element.9), channel_id=1, source_target_pairs={{1,0},{2,1},{3,2},{4,3},{5,4},{6,5},{7,6},{9,8},{10,9},{11,10},{12... | collective-permute-start | bytes 63848 | tf_op jit(solution)/shard_map/ppermute | solution.py:21
  18.6 14.8 %collective-permute-start.2 = (f32[532,10]{1,0:T(8,128)S(1)}, f32[532,10]{1,0:T(8,128)S(1)}, u32[]{:S(2)}, u32[]{:S(2)}) collective-permute-start(f32[532,10]{1,0:T(8,128)S(1)} %get-tuple-element.8), channel_id=1, source_target_pairs={{0,1},{1,2},{2,3},{3,4},{4,5},{5,6},{6,7},{8,9},{9,10},{10,11},{11... | collective-permute-start | bytes 63848 | tf_op jit(solution)/shard_map/ppermute | solution.py:20
  70.1 249.9 %all-gather.6.cloned.1.call-start = ((), (), s32[]{:S(2)}) async-start(), calls=%async_computation.1 | async-start | bytes 9437184 | tf_op jit(solution)/shard_map/all_gather | solution.py:74
  108.3 337.0 %all-gather.4.cloned.1.call-start = ((), (), s32[]{:S(2)}) async-start(), calls=%async_computation | async-start | bytes 9437184 | tf_op jit(solution)/shard_map/all_gather | solution.py:73
  154.6 6.4 %copy-start.3 = (s32[1,32]{1,0:T(1,128)S(1)}, s32[1,32]{1,0:T(1,128)}, u32[]{:S(2)}) copy-start(s32[1,32]{1,0:T(1,128)} %param.11) | copy-start | bytes 388
  185.3 9.7 %copy-start.2 = (f32[8,4,3,3]{0,1,3,2:T(4,128)S(1)}, f32[8,4,3,3]{0,1,3,2:T(4,128)}, u32[]{:S(2)}) copy-start(f32[8,4,3,3]{0,1,3,2:T(4,128)} %param.13) | copy-start | bytes 3460
Sparse Core Ops, SparseCore 0:
  70.2 124.3 all-gather.7
  196.8 123.0 all-gather.5
  322.1 123.0 all-gather.3
where the time goes:
time: 471 us; the launch traced here: 468 us
  waiting for transfers between devices  260 us (55%)
  other arithmetic  136 us (29%)
  local copies, waits for them, and re-layouts  38.8 us (8%)
  between operations  13.3 us (3%)
  starting transfers between devices  12.1 us (3%)
  matrix products  8.5 us (2%)
    all_gather x1, waiting for transfers between devices, on_device(): lax.all_gather(smoothed[0], 'tile', axis=1, tiled=True)  125 us
    all_gather x1, waiting for transfers between devices, on_device(): lax.all_gather(smoothed[1], 'tile', axis=1, tiled=True)  124 us
    add x3, other arithmetic, smooth(): result = result + gauss[offset] * across[:, offset:offset + out_cols]  58.4 us
    add x3, other arithmetic, smooth(): across = across + gauss[offset] * padded[offset:offset + out_rows, :]  49.3 us
    broadcast_in_dim x1, other arithmetic, on_device(): return difference[None]  16.6 us
  transfers between devices with their start and end apart: 7, of which 4 were waited for; matrix products, arithmetic and copies ran while one was open for 27% of the time, Pallas kernels for 0%

commit v1 on v0

v1 whole, which is shorter than its diff:
```python
import functools

import jax
import jax.numpy as jnp
import ml_dtypes
import numpy as np
from jax import lax
from jax.experimental import pallas as pl
from jax.experimental.pallas import tpu as pltpu
from jax.sharding import PartitionSpec as P

HALF = 10
KSETS = 4
SIGMAS = (1.5, 3.0, 5.0)
HALO = 16
EDGE = 128
BAND = 128
CHUNKS = 2
LINES = 128


def basis_taps():
    positions = np.arange(-HALF, HALF + 1).astype(np.float64)
    kernels = []
    for sigma_value in SIGMAS:
        gauss = np.exp(-0.5 * (positions / sigma_value) ** 2)
        kernels.append(gauss / np.sum(gauss))
    return kernels


def banded(taps, rows, cols, shift):
    distance = np.arange(cols)[None, :] - np.arange(rows)[:, None] - shift
    inside = np.abs(distance) <= HALF
    return np.where(inside, taps[np.clip(distance + HALF, 0, 2 * HALF)], 0.0)


def smoothing_matrices(patch_cols):
    down, across, gains = [], [], []
    for taps in basis_taps():
        near = taps.astype(ml_dtypes.bfloat16)
        down.append(banded(taps, BAND, BAND + 2 * HALO, HALO))
        across.append(banded(taps, patch_cols, patch_cols + 2 * EDGE, EDGE))
        gains.append(1.0 / np.sum(near.astype(np.float64)) ** 2)
    as_bf16 = lambda parts: np.stack(parts).astype(ml_dtypes.bfloat16)
    return np.concatenate(list(as_bf16(down)), axis=0), as_bf16(across), gains


def inner_size(count):
    best = 1
    for size in range(1, count + 1):
        if count % size == 0 and size * size <= count:
            best = size
    return best


def arrival_codes(count):
    inner = inner_size(count)
    codes = []
    for me in range(count):
        z, x = divmod(me, inner)
        near = sorted(range(count // inner), key=lambda other: (abs(other - z), other))
        keys = []
        for q in range(count):
            if q == me:
                continue
            qz, qx = divmod(q, inner)
            away = abs(qz - z)
            time = away if qx == x else max(near.index(qz), away) + abs(qx - x)
            keys.append((time, qx != x, q))
        order = [q for _, _, q in sorted(keys)]
        words = []
        for first in range(0, count - 1, 7):
            words.append(sum(q << (4 * i) for i, q in enumerate(order[first : first + 7])))
        codes.append(words)
    return codes


def model_kernel(
    count, ccd_count, template, weights, down, across, out,
    strip, load_sem, send_sem, recv_sem, hsend_sem, hrecv_sem,
):
    me = lax.axis_index("tile")
    row = lax.axis_index("ccd")
    inner = inner_size(count)
    outer = count // inner
    z, x = me // inner, me % inner
    rows, patch_cols = template.shape
    cols = out.shape[1]
    part = rows // CHUNKS

    targets = (me - inner, me + inner, me - 1, me + 1)
    there = (z > 0, z < outer - 1, x > 0, x < inner - 1)
    halo_there = (row > 0, row < ccd_count - 1)

    load = pltpu.make_async_copy(template, strip.at[me, pl.ds(HALO, rows)], load_sem)
    load.start()

    barrier = pltpu.get_barrier_semaphore()
    total = jnp.int32(0)
    for target, exists in zip(targets, there):
        @pl.when(exists)
        def _():
            pl.semaphore_signal(barrier, inc=1, device_id=(row, target))
        total = total + exists.astype(jnp.int32)
    for step, exists in zip((-1, 1), halo_there):
        @pl.when(exists)
        def _():
            pl.semaphore_signal(barrier, inc=1, device_id=(row + step, me))
        total = total + exists.astype(jnp.int32)
    pl.semaphore_wait(barrier, total)

    def send(q, c, d, own):
        piece = pl.ds(HALO + c * part, part)
        return pltpu.make_async_remote_copy(
            src_ref=template.at[pl.ds(c * part, part)] if own else strip.at[q, piece],
            dst_ref=strip.at[q, piece],
            send_sem=send_sem.at[d, q, c],
            recv_sem=recv_sem.at[q, c],
            device_id=(row, targets[d]),
        )

    def halo(q, d):
        source = pl.ds(HALO, HALO) if d == 0 else pl.ds(rows, HALO)
        target = pl.ds(HALO + rows, HALO) if d == 0 else pl.ds(0, HALO)
        return pltpu.make_async_remote_copy(
            src_ref=strip.at[q, source],
            dst_ref=strip.at[q, target],
            send_sem=hsend_sem.at[d, q],
            recv_sem=hrecv_sem.at[d, q],
            device_id=(row + (-1 if d == 0 else 1), me),
        )

    def routes(q):
        qz, qx = q // inner, q % inner
        same = qx == x
        return (
            same & (qz > z) & there[0],
            same & (qz < z) & there[1],
            ((qx > x) | same) & there[2],
            ((qx < x) | same) & there[3],
        )

    for c in range(CHUNKS):
        for d in range(4):
            @pl.when(there[d])
            def _():
                send(me, c, d, True).start()
    load.wait()
    for d in range(2):
        @pl.when(halo_there[d])
        def _():
            halo(me, d).start()

    @pl.when(row == 0)
    def _():
        for q in range(count):
            strip[q, 0:HALO, :] = jnp.zeros((HALO, patch_cols), jnp.float32)

    @pl.when(row == ccd_count - 1)
    def _():
        for q in range(count):
            strip[q, rows + HALO : rows + 2 * HALO, :] = jnp.zeros((HALO, patch_cols), jnp.float32)

    out[...] = jnp.zeros_like(out)

    def add_model(q):
        first = pl.multiple_of(q * patch_cols, EDGE)
        wide = patch_cols + 2 * EDGE
        left = pl.multiple_of(jnp.maximum(first - EDGE, 0), EDGE)
        right = pl.multiple_of(jnp.minimum(first + patch_cols, cols - EDGE), EDGE)

        def band(r, carry):
            at = pl.multiple_of(r * BAND, BAND)
            lines = pl.ds(at, BAND)
            pixel = strip[q, pl.ds(at, BAND + 2 * HALO), :].astype(jnp.bfloat16)
            tall = jnp.dot(down[...], pixel, preferred_element_type=jnp.float32)
            tall = tall.astype(jnp.bfloat16)
            v = (
                lax.broadcasted_iota(jnp.int32, (BAND, wide), 0) + r * BAND
            ).astype(jnp.float32) * (2.0 / rows) - (rows - 1) / rows
            model = None
            for b in range(3):
                flat = jnp.dot(
                    tall[b * BAND : (b + 1) * BAND], across[b], preferred_element_type=jnp.float32
                )
                const = weights[b : b + 1, pl.ds(first, wide)]
                slope = weights[3 + b : 4 + b, pl.ds(first, wide)]
                term = (const + slope * v) * flat
                model = term if model is None else model + term
            out[lines, pl.ds(first, patch_cols)] += model[:, EDGE : EDGE + patch_cols]
            out[lines, pl.ds(left, EDGE)] += model[:, :EDGE]
            out[lines, pl.ds(right, EDGE)] += model[:, EDGE + patch_cols :]
            return carry

        lax.fori_loop(0, rows // BAND, band, 0)

    def halos_in(q):
        for d in range(2):
            @pl.when(halo_there[1 - d])
            def _():
                halo(q, d).wait_recv()

    halos_in(me)
    add_model(me)

    table = arrival_codes(count)
    words = []
    for w in range(len(table[0])):
        word = jnp.int32(0)
        for i in range(count):
            word = jnp.where(me == i, jnp.int32(table[i][w]), word)
        words.append(word)

    def arrive(_, words):
        words = list(words)
        q = words[0] % 16
        for w in range(len(words)):
            words[w] = words[w] // 16
            if w + 1 < len(words):
                words[w] = words[w] + (words[w + 1] % 16) * (1 << 24)
        onward = routes(q)
        for c in range(CHUNKS):
            send(q, c, 0, False).wait_recv()
            for d in range(4):
                @pl.when(onward[d])
                def _():
                    send(q, c, d, False).start()
        for d in range(2):
            @pl.when(halo_there[d])
            def _():
                halo(q, d).start()
        halos_in(q)
        add_model(q)
        return tuple(words)

    lax.fori_loop(0, count - 1, arrive, tuple(words))

    def drain(q, carry):
        onward = routes(q)
        for d in range(4):
            @pl.when(jnp.where(q == me, there[d], onward[d]))
            def _():
                for c in range(CHUNKS):
                    send(q, c, d, False).wait_send()
        for d in range(2):
            @pl.when(halo_there[d])
            def _():
                halo(q, d).wait_send()
        return carry

    lax.fori_loop(0, count, drain, 0)


def difference_kernel(offsets, exposure, mats, model, weights, out, pixels):
    blocks, depth, block = mats.shape
    pixels[...] = exposure[...].astype(jnp.bfloat16)
    for j in range(blocks):
        start = pl.multiple_of(offsets[j] * block, block)
        value = jnp.dot(
            pixels[:, pl.ds(start, depth)], mats[j], preferred_element_type=jnp.float32
        )
        here = slice(j * block, (j + 1) * block)
        covered = weights[6:7, EDGE + j * block : EDGE + (j + 1) * block]
        out[:, here] = value * covered - model[:, here]


def on_device(exposures, interp, col_offsets, template, coef_table, coef_index, intersection):
    rows, cols = exposures.shape[1:]
    patch_cols = template.shape[1]
    count, ccd_count = lax.axis_size("tile"), lax.axis_size("ccd")
    patch_row = lax.axis_index("ccd")
    my_epoch = lax.axis_index("tile")
    down, across, gains = smoothing_matrices(patch_cols)

    set_ids = coef_index[my_epoch, patch_row]
    set_pick = (set_ids[:, None] == jnp.arange(KSETS)[None, :]).astype(jnp.float32)
    coef = jnp.sum(set_pick[:, :, None, None] * coef_table[my_epoch][None], axis=1)
    covered = intersection[my_epoch, patch_row].astype(jnp.float32)
    coef = coef * covered[:, None, None] * jnp.asarray(gains, jnp.float32)[None, :, None]
    u = (jnp.arange(patch_cols).astype(jnp.float32) - (patch_cols - 1) / 2.0) / (patch_cols / 2.0)
    spread = coef.transpose(1, 2, 0)[:, :, :, None]
    const = (spread[:, 0] + spread[:, 1] * u[None, None, :]).reshape(3, cols)
    slope = jnp.broadcast_to(spread[:, 2], (3, count, patch_cols)).reshape(3, cols)
    cover = jnp.broadcast_to(covered[None, :, None], (2, count, patch_cols)).reshape(2, cols)
    weights = jnp.pad(jnp.concatenate([const, slope, cover]), ((0, 0), (EDGE, EDGE)))

    anywhere = pl.BlockSpec(memory_space=pl.ANY)
    vmem = pl.BlockSpec(memory_space=pltpu.VMEM)
    model = pl.pallas_call(
        functools.partial(model_kernel, count, ccd_count),
        out_shape=jax.ShapeDtypeStruct((rows, cols), jnp.float32),
        in_specs=[anywhere, vmem, vmem, vmem],
        out_specs=vmem,
        scratch_shapes=[
            pltpu.VMEM((count, rows + 2 * HALO, patch_cols), jnp.float32),
            pltpu.SemaphoreType.DMA,
            pltpu.SemaphoreType.DMA((4, count, CHUNKS)),
            pltpu.SemaphoreType.DMA((count, CHUNKS)),
            pltpu.SemaphoreType.DMA((2, count)),
            pltpu.SemaphoreType.DMA((2, count)),
        ],
        compiler_params=pltpu.CompilerParams(
            collective_id=0, has_side_effects=True, vmem_limit_bytes=32 * 2**20
        ),
    )(template, weights, down, across)

    blocks, depth, block = interp.shape[1:]
    lines = min(LINES, rows)
    result = pl.pallas_call(
        difference_kernel,
        grid=(rows // lines,),
        out_shape=jax.ShapeDtypeStruct((rows, cols), jnp.float32),
        in_specs=[
            pl.BlockSpec(memory_space=pltpu.SMEM),
            pl.BlockSpec((lines, cols), lambda i: (i, 0)),
            pl.BlockSpec((blocks, depth, block), lambda i: (0, 0, 0)),
            pl.BlockSpec((lines, cols), lambda i: (i, 0)),
            pl.BlockSpec(weights.shape, lambda i: (0, 0)),
        ],
        out_specs=pl.BlockSpec((lines, cols), lambda i: (i, 0)),
        scratch_shapes=[pltpu.VMEM((lines, cols), jnp.bfloat16)],
        compiler_params=pltpu.CompilerParams(vmem_limit_bytes=32 * 2**20),
    )(col_offsets[0], exposures[0], interp[0], model, weights)
    return result[None]


def solution(mesh):
    placed = (
        P("tile", "ccd", None),
        P("tile", None, None, None),
        P("tile", None),
        P("ccd", "tile"),
        P(),
        P(),
        P(),
    )
    return jax.shard_map(
        on_device, mesh=mesh, in_specs=placed, out_specs=P("tile", "ccd", None), check_vma=False
    )
```

time: 471 us -> 115 us (0.24)
  waiting for transfers between devices: 260 us -> 0 us
  other arithmetic: 136 us -> 1.8 us
  Pallas kernels: 0 us -> 108 us
  local copies, waits for them, and re-layouts: 38.8 us -> 4.88 us
  between operations: 13.3 us -> 0.12 us
  starting transfers between devices: 12.1 us -> 0 us
  matrix products: 8.5 us -> 0 us
    all_gather x3 -> x0, waiting for transfers between devices: 249 us -> none  [the longest x1 125 us: on_device(): lax.all_gather(smoothed[0], 'tile', axis=1, tiled=True)]
    add x9 -> x1, other arithmetic: 108 us -> 0.03 us  [on_device(): const = (spread[:, 0] + spread[:, 1] * u[None, None, :]).reshape(3, cols)]
    pallas_call x0 -> x2, Pallas kernels: none -> 108 us  [the longest x1 102 us: on_device(): pl.pallas_call(functools.partial(model_kernel, count, ccd_count), out_sha...]
    broadcast_in_dim x1, other arithmetic: 16.6 us -> 0.88 us  [on_device(): spread = coef.transpose(1, 2, 0)[:, :, :, None]]
    ppermute x4 -> x0, starting transfers between devices: 11.9 us -> none  [the longest x2 8.5 us: extended(): before = lax.ppermute(last, axis, up)]
    gather x2 -> x0, local copies, waits for them, and re-layouts: 10.5 us -> none  [the longest x1 5.29 us: resample(): second_part = jnp.take(tiles, offsets + 1, axis=1)]
    ppermute x4 -> x0, waiting for transfers between devices: 10.2 us -> none  [the longest x2 6.64 us: extended(): before = lax.ppermute(last, axis, up)]
    reshape x2 -> x0, local copies, waits for them, and re-layouts: 9.04 us -> none  [the longest x1 8.93 us: resample(): return output.reshape(row_count, block_count * block_cols)]
  transfers between devices with their start and end apart: 7 -> 0, of which waited for: 4 -> 0; matrix products, arithmetic and copies ran while one was open for 27% -> 0% of each run, Pallas kernels for 0% -> 0%
where the time goes in v1:
time: 115 us; the launch traced here: 114 us
  Pallas kernels  108 us (94%)
  local copies, waits for them, and re-layouts  4.88 us (4%)
  other arithmetic  1.8 us (2%)
    pallas_call x1, Pallas kernels, on_device(): pl.pallas_call(functools.partial(model_kernel, count, ccd_count), out_sha...  102 us
    pallas_call x1, Pallas kernels, on_device(): pl.pallas_call(difference_kernel, grid=(rows // lines,), out_shape=jax.Sh...  5.81 us
    unnamed x27, local copies, waits for them, and re-layouts  4.63 us

profile of v1, /device:TPU:1, one launch (start us, length us, event | category | flops | bytes accessed | tf_op | source)
XLA Modules:
  0.0 114.4 jit_solution(2585528335217566224)
XLA Ops:
  0.0 0.0 copy-start
  0.0 0.0 copy-start.6
  0.0 0.7 fusion.2
  0.8 0.1 broadcast_bitcast_fusion.3
  0.9 0.0 copy-done
  0.9 0.1 constant_dynamic-slice_fusion.1
  1.0 0.2 copy.15
  1.1 0.0 copy-start.1
  1.1 0.1 multiply_reduce_fusion
  1.2 0.9 multiply_bitcast_fusion
  2.1 0.1 broadcast_bitcast_fusion.2
  2.2 0.1 broadcast_bitcast_fusion
  2.4 0.1 broadcast_bitcast_fusion.1
  2.6 0.0 copy-start.2
  2.6 2.0 %copy-done.2 = bf16[3,512,768]{2,1,0:T(8,128)(2,1)S(1)} copy-done((bf16[3,512,768]{2,1,0:T(8,128)(2,1)S(1)}, bf16[3,512,768]{2,1,0:T(8,128)(2,1)}, u32[]{:S(2)}) %copy-start.2) | copy-done | bytes 2359320
  4.6 0.0 copy-start.4
  4.6 1.2 %copy-done.4 = f32[512,512]{1,0:T(8,128)S(1)} copy-done((f32[512,512]{1,0:T(8,128)S(1)}, f32[512,512]{1,0:T(8,128)}, u32[]{:S(2)}) %copy-start.4) | copy-done | bytes 1048600
  5.8 0.0 copy-start.5
  5.8 0.9 copy-done.5
  6.8 0.0 copy-start.3
  6.8 101.7 %shard_map.100.model = f32[512,4096]{1,0:T(8,128)S(1)} custom-call(f32[512,512]{1,0:T(8,128)S(1)} %copy-done.4, f32[8,4352]{1,0:T(8,128)S(1)} %select_maximum_fusion.weights, bf16[384,160]{1,0:T(8,128)(2,1)S(1)} %copy-done.5, bf16[3,512,768]{2,1,0:T(8,128)(2,1)S(1)} %copy-done.2), custom_call_target="tpu_custom_call" | custom-call | tf_op jit(solution)/shard_map/pallas_call | solution.py:289
  108.5 0.0 copy-done.6
  108.5 0.0 copy-done.1
  108.5 0.0 copy-done.3
  108.5 5.8 %shard_map.101 = f32[512,4096]{1,0:T(8,128)} custom-call(s32[32]{0:T(128)S(1)} %bitcast.40, f32[512,4096]{1,0:T(8,128)S(1)} %bitcast.38, bf16[32,256,128]{2,1,0:T(8,128)(2,1)S(1)} %bitcast.39, f32[512,4096]{1,0:T(8,128)S(1)} %shard_map.100.model, f32[8,4352]{1,0:T(8,128)S(1)} %select_maximum_fusion.weights), custom_call_target="tpu_custom_call" | custom-call | tf_op jit(solution)/shard_map/pallas_call | solution.py:309
  (15 shorter events, 0.3 us)
Async XLA Ops:
  0.0 0.9 copy-start
  0.0 108.5 %copy-start.6 = (s32[1,32]{1,0:T(1,128)S(1)}, s32[1,32]{1,0:T(1,128)}, u32[]{:S(2)}) copy-start(s32[1,32]{1,0:T(1,128)} %param.12) | copy-start | bytes 388
  1.1 107.4 %copy-start.1 = (f32[1,512,4096]{2,1,0:T(8,128)S(1)}, f32[1,512,4096]{2,1,0:T(8,128)}, u32[]{:S(2)}) copy-start(f32[1,512,4096]{2,1,0:T(8,128)} %param.10) | copy-start | bytes 25165828
  2.6 2.0 %copy-start.2 = (bf16[3,512,768]{2,1,0:T(8,128)(2,1)S(1)}, bf16[3,512,768]{2,1,0:T(8,128)(2,1)}, u32[]{:S(2)}) copy-start(bf16[3,512,768]{2,1,0:T(8,128)(2,1)} %constant.31.clone.across) | copy-start | bytes 7077892
  4.6 1.2 %copy-start.4 = (f32[512,512]{1,0:T(8,128)S(1)}, f32[512,512]{1,0:T(8,128)}, u32[]{:S(2)}) copy-start(f32[512,512]{1,0:T(8,128)} %template.1) | copy-start | bytes 3145732
  5.8 0.9 copy-start.5
  6.8 101.8 %copy-start.3 = (bf16[1,32,256,128]{3,2,1,0:T(8,128)(2,1)S(1)}, bf16[1,32,256,128]{3,2,1,0:T(8,128)(2,1)}, u32[]{:S(2)}) copy-start(bf16[1,32,256,128]{3,2,1,0:T(8,128)(2,1)} %param.11) | copy-start | bytes 6291460

commit v2 on v1

--- a/solution.py
+++ b/solution.py
@@ -1,4 +1,5 @@
 import functools
+import heapq
 
 import jax
 import jax.numpy as jnp
@@ -15,7 +16,7 @@
 HALO = 16
 EDGE = 128
 BAND = 128
-CHUNKS = 2
+CHUNKS = 4
 LINES = 128
 
 
@@ -28,21 +29,21 @@
     return kernels
 
 
-def banded(taps, rows, cols, shift):
-    distance = np.arange(cols)[None, :] - np.arange(rows)[:, None] - shift
-    inside = np.abs(distance) <= HALF
-    return np.where(inside, taps[np.clip(distance + HALF, 0, 2 * HALF)], 0.0)
-
-
-def smoothing_matrices(patch_cols):
-    down, across, gains = [], [], []
-    for taps in basis_taps():
-        near = taps.astype(ml_dtypes.bfloat16)
-        down.append(banded(taps, BAND, BAND + 2 * HALO, HALO))
-        across.append(banded(taps, patch_cols, patch_cols + 2 * EDGE, EDGE))
-        gains.append(1.0 / np.sum(near.astype(np.float64)) ** 2)
-    as_bf16 = lambda parts: np.stack(parts).astype(ml_dtypes.bfloat16)
-    return np.concatenate(list(as_bf16(down)), axis=0), as_bf16(across), gains
+def smoothing_gains():
+    near = [taps.astype(ml_dtypes.bfloat16).astype(np.float64) for taps in basis_taps()]
+    return [1.0 / np.sum(taps) ** 2 for taps in near]
+
+
+def banded(b, rows, cols, shift, first=0):
+    shape = (rows, cols)
+    distance = (
+        lax.broadcasted_iota(jnp.int32, shape, 1)
+        - lax.broadcasted_iota(jnp.int32, shape, 0)
+        - (shift + first)
+    )
+    away = distance.astype(jnp.float32)
+    taps = jnp.exp(away * away * (-0.5 / SIGMAS[b] ** 2)) * basis_taps()[b][HALF]
+    return jnp.where(jnp.abs(away) <= HALF, taps, 0.0).astype(jnp.bfloat16)
 
 
 def inner_size(count):
@@ -53,31 +54,70 @@
     return best
 
 
+def routes(outer, inner, me, q, c):
+    z, x = divmod(me, inner)
+    qz, qx = divmod(q, inner)
+    detour = inner == 2 and outer > 2 and c >= CHUNKS // 2 and qz in (0, outer - 1)
+    along = qx == x or detour
+    return (
+        along and qz >= z > 0,
+        along and qz <= z < outer - 1,
+        (q == me or (not detour and qx >= x)) and x > 0,
+        (q == me or (not detour and qx <= x)) and x < inner - 1,
+    )
+
+
+def arrival_events(count):
+    inner = inner_size(count)
+    outer = count // inner
+    steps = (-inner, inner, -1, 1)
+    queue, free, tick = [], {}, 0
+    seen = [[] for _ in range(count)]
+    for q in range(count):
+        for d in range(4):
+            for c in range(CHUNKS) if d < 2 else reversed(range(CHUNKS)):
+                if routes(outer, inner, q, q, c)[d]:
+                    heapq.heappush(queue, (0, tick, q, d, q, c))
+                    tick += 1
+    while queue:
+        ready, _, me, d, q, c = heapq.heappop(queue)
+        if ready < free.get((me, d), 0):
+            heapq.heappush(queue, (free[me, d], tick, me, d, q, c))
+            tick += 1
+            continue
+        free[me, d] = ready + 1
+        there = me + steps[d]
+        seen[there].append((ready + 1, tick, q * CHUNKS + c))
+        for onward in range(4):
+            if routes(outer, inner, there, q, c)[onward]:
+                heapq.heappush(queue, (ready + 1, tick, there, onward, q, c))
+                tick += 1
+    return [[event for _, _, event in sorted(arrivals)] for arrivals in seen]
+
+
+DIGIT = 256
+PER_WORD = 3
+
+
 def arrival_codes(count):
-    inner = inner_size(count)
     codes = []
-    for me in range(count):
-        z, x = divmod(me, inner)
-        near = sorted(range(count // inner), key=lambda other: (abs(other - z), other))
-        keys = []
-        for q in range(count):
-            if q == me:
-                continue
-            qz, qx = divmod(q, inner)
-            away = abs(qz - z)
-            time = away if qx == x else max(near.index(qz), away) + abs(qx - x)
-            keys.append((time, qx != x, q))
-        order = [q for _, _, q in sorted(keys)]
-        words = []
-        for first in range(0, count - 1, 7):
-            words.append(sum(q << (4 * i) for i, q in enumerate(order[first : first + 7])))
-        codes.append(words)
+    for events in arrival_events(count):
+        assert len(events) == (count - 1) * CHUNKS
+        left = {q: CHUNKS for q in range(count)}
+        digits = []
+        for event in events:
+            left[event // CHUNKS] -= 1
+            digits.append(event * 2 + (left[event // CHUNKS] == 0))
+        codes.append([
+            sum(int(v) * DIGIT**i for i, v in enumerate(digits[first : first + PER_WORD]))
+            for first in range(0, len(digits), PER_WORD)
+        ])
     return codes
 
 
 def model_kernel(
-    count, ccd_count, template, weights, down, across, out,
-    strip, load_sem, send_sem, recv_sem, hsend_sem, hrecv_sem,
+    count, ccd_count, template, weights, out,
+    strip, down, across, load_sem, send_sem, recv_sem, hsend_sem, hrecv_sem,
 ):
     me = lax.axis_index("tile")
     row = lax.axis_index("ccd")
@@ -110,7 +150,7 @@
     pl.semaphore_wait(barrier, total)
 
     def send(q, c, d, own):
-        piece = pl.ds(HALO + c * part, part)
+        piece = pl.ds(pl.multiple_of(HALO + c * part, HALO), part)
         return pltpu.make_async_remote_copy(
             src_ref=template.at[pl.ds(c * part, part)] if own else strip.at[q, piece],
             dst_ref=strip.at[q, piece],
@@ -130,18 +170,8 @@
             device_id=(row + (-1 if d == 0 else 1), me),
         )
 
-    def routes(q):
-        qz, qx = q // inner, q % inner
-        same = qx == x
-        return (
-            same & (qz > z) & there[0],
-            same & (qz < z) & there[1],
-            ((qx > x) | same) & there[2],
-            ((qx < x) | same) & there[3],
-        )
-
-    for c in range(CHUNKS):
-        for d in range(4):
+    for d in (0, 2, 1, 3):
+        for c in range(CHUNKS) if d < 2 else reversed(range(CHUNKS)):
             @pl.when(there[d])
             def _():
                 send(me, c, d, True).start()
@@ -161,7 +191,11 @@
         for q in range(count):
             strip[q, rows + HALO : rows + 2 * HALO, :] = jnp.zeros((HALO, patch_cols), jnp.float32)
 
-    out[...] = jnp.zeros_like(out)
+    def clear(r, carry):
+        out[pl.ds(pl.multiple_of(r * HALO, HALO), HALO), :] = jnp.zeros((HALO, cols), jnp.float32)
+        return carry
+
+    lax.fori_loop(0, rows // HALO, clear, 0)
 
     def add_model(q):
         first = pl.multiple_of(q * patch_cols, EDGE)
@@ -200,8 +234,35 @@
             def _():
                 halo(q, d).wait_recv()
 
+    for b in range(3):
+        down[b * BAND : (b + 1) * BAND, :] = banded(b, BAND, BAND + 2 * HALO, HALO)
+
+        def fill(i, carry):
+            first = pl.multiple_of(i * HALO, HALO)
+            across[b, pl.ds(first, HALO), :] = banded(
+                b, HALO, patch_cols + 2 * EDGE, EDGE, i * HALO
+            )
+            return carry
+
+        lax.fori_loop(0, patch_cols // HALO, fill, 0)
+
     halos_in(me)
     add_model(me)
+
+    def paths(q, c):
+        qz, qx = q // inner, q % inner
+        detour = jnp.zeros((), jnp.bool_)
+        if inner == 2 and outer > 2:
+            detour = (c >= CHUNKS // 2) & ((qz == 0) | (qz == outer - 1))
+        own = q == me
+        along = (qx == x) | detour
+        level = jnp.logical_not(detour)
+        return (
+            along & (qz >= z) & there[0],
+            along & (qz <= z) & there[1],
+            (own | level & (qx >= x)) & there[2],
+            (own | level & (qx <= x)) & there[3],
+        )
 
     table = arrival_codes(count)
     words = []
@@ -213,42 +274,47 @@
 
     def arrive(_, words):
         words = list(words)
-        q = words[0] % 16
+        digit = words[0] % DIGIT
         for w in range(len(words)):
-            words[w] = words[w] // 16
+            words[w] = words[w] // DIGIT
             if w + 1 < len(words):
-                words[w] = words[w] + (words[w + 1] % 16) * (1 << 24)
-        onward = routes(q)
-        for c in range(CHUNKS):
-            send(q, c, 0, False).wait_recv()
-            for d in range(4):
-                @pl.when(onward[d])
-                def _():
-                    send(q, c, d, False).start()
+                words[w] = words[w] + (words[w + 1] % DIGIT) * DIGIT ** (PER_WORD - 1)
+        done, event = digit % 2, digit // 2
+        q, c = event // CHUNKS, event % CHUNKS
+        send(q, c, 0, False).wait_recv()
+        onward = paths(q, c)
+        for d in range(4):
+            @pl.when(onward[d])
+            def _():
+                send(q, c, d, False).start()
         for d in range(2):
-            @pl.when(halo_there[d])
+            @pl.when((c == (0 if d == 0 else CHUNKS - 1)) & halo_there[d])
             def _():
                 halo(q, d).start()
-        halos_in(q)
-        add_model(q)
+
+        @pl.when(done == 1)
+        def _():
+            halos_in(q)
+            add_model(q)
+
         return tuple(words)
 
-    lax.fori_loop(0, count - 1, arrive, tuple(words))
-
-    def drain(q, carry):
-        onward = routes(q)
+    lax.fori_loop(0, (count - 1) * CHUNKS, arrive, tuple(words))
+
+    def drain(event, carry):
+        q, c = event // CHUNKS, event % CHUNKS
+        onward = paths(q, c)
         for d in range(4):
-            @pl.when(jnp.where(q == me, there[d], onward[d]))
-            def _():
-                for c in range(CHUNKS):
-                    send(q, c, d, False).wait_send()
+            @pl.when(onward[d])
+            def _():
+                send(q, c, d, False).wait_send()
         for d in range(2):
-            @pl.when(halo_there[d])
+            @pl.when((c == 0) & halo_there[d])
             def _():
                 halo(q, d).wait_send()
         return carry
 
-    lax.fori_loop(0, count, drain, 0)
+    lax.fori_loop(0, count * CHUNKS, drain, 0)
 
 
 def difference_kernel(offsets, exposure, mats, model, weights, out, pixels):
@@ -270,7 +336,7 @@
     count, ccd_count = lax.axis_size("tile"), lax.axis_size("ccd")
     patch_row = lax.axis_index("ccd")
     my_epoch = lax.axis_index("tile")
-    down, across, gains = smoothing_matrices(patch_cols)
+    gains = smoothing_gains()
 
     set_ids = coef_index[my_epoch, patch_row]
     set_pick = (set_ids[:, None] == jnp.arange(KSETS)[None, :]).astype(jnp.float32)
@@ -284,15 +350,17 @@
     cover = jnp.broadcast_to(covered[None, :, None], (2, count, patch_cols)).reshape(2, cols)
     weights = jnp.pad(jnp.concatenate([const, slope, cover]), ((0, 0), (EDGE, EDGE)))
 
-    anywhere = pl.BlockSpec(memory_space=pl.ANY)
+    in_hbm = pl.BlockSpec(memory_space=pltpu.HBM)
     vmem = pl.BlockSpec(memory_space=pltpu.VMEM)
     model = pl.pallas_call(
         functools.partial(model_kernel, count, ccd_count),
         out_shape=jax.ShapeDtypeStruct((rows, cols), jnp.float32),
-        in_specs=[anywhere, vmem, vmem, vmem],
+        in_specs=[in_hbm, vmem],
         out_specs=vmem,
         scratch_shapes=[
             pltpu.VMEM((count, rows + 2 * HALO, patch_cols), jnp.float32),
+            pltpu.VMEM((3 * BAND, BAND + 2 * HALO), jnp.bfloat16),
+            pltpu.VMEM((3, patch_cols, patch_cols + 2 * EDGE), jnp.bfloat16),
             pltpu.SemaphoreType.DMA,
             pltpu.SemaphoreType.DMA((4, count, CHUNKS)),
             pltpu.SemaphoreType.DMA((count, CHUNKS)),
@@ -302,7 +370,7 @@
         compiler_params=pltpu.CompilerParams(
             collective_id=0, has_side_effects=True, vmem_limit_bytes=32 * 2**20
         ),
-    )(template, weights, down, across)
+    )(template, weights)
 
     blocks, depth, block = interp.shape[1:]
     lines = min(LINES, rows)

time: 115 us -> 146 us (1.27)
  the two profiles are of different devices: /device:TPU:1 before, /device:TPU:29 now
where the time goes in v2:
time: 146 us
  Pallas kernels  142 us (97%)
  local copies, waits for them, and re-layouts  2.29 us (2%)
  other arithmetic  1.92 us (1%)
    pallas_call x1, Pallas kernels, on_device(): pl.pallas_call(functools.partial(model_kernel, count, ccd_count), out_sha...  136 us
    pallas_call x1, Pallas kernels, on_device(): pl.pallas_call(difference_kernel, grid=(rows // lines,), out_shape=jax.Sh...  5.84 us

profile of v2, /device:TPU:29, one launch (start us, length us, event | category | flops | bytes accessed | tf_op | source)
XLA Modules:
  0.0 146.0 jit_solution(1172687145634648465)
XLA Ops:
  0.0 0.0 copy-start
  0.0 0.0 copy-start.2
  0.0 0.9 fusion.2
  0.9 0.1 broadcast_bitcast_fusion.3
  1.0 0.0 copy-done
  1.0 0.1 constant_dynamic-slice_fusion.1
  1.1 0.2 copy.13
  1.2 0.0 copy-start.1
  1.2 0.1 multiply_reduce_fusion
  1.3 0.9 multiply_bitcast_fusion
  2.3 0.1 broadcast_bitcast_fusion.2
  2.4 0.1 broadcast_bitcast_fusion
  2.5 0.1 broadcast_bitcast_fusion.1
  2.7 0.0 copy-start.3
  2.7 1.6 %copy-done.3 = f32[512,512]{1,0:T(8,128)S(1)} copy-done((f32[512,512]{1,0:T(8,128)S(1)}, f32[512,512]{1,0:T(8,128)}, u32[]{:S(2)}) %copy-start.3) | copy-done | bytes 1048600
  4.3 0.0 copy-start.4
  4.3 135.8 %shard_map.82.model = f32[512,4096]{1,0:T(8,128)S(1)} custom-call(f32[512,512]{1,0:T(8,128)S(1)} %copy-done.3, f32[8,4352]{1,0:T(8,128)S(1)} %select_maximum_fusion.weights), custom_call_target="tpu_custom_call" | custom-call | tf_op jit(solution)/shard_map/pallas_call | solution.py:355
  140.1 0.0 copy-done.2
  140.1 0.0 copy-done.1
  140.1 0.0 copy-done.4
  140.1 5.8 %shard_map.83 = f32[512,4096]{1,0:T(8,128)} custom-call(s32[32]{0:T(128)S(1)} %bitcast.40, f32[512,4096]{1,0:T(8,128)S(1)} %bitcast.38, bf16[32,256,128]{2,1,0:T(8,128)(2,1)S(1)} %bitcast.39, f32[512,4096]{1,0:T(8,128)S(1)} %shard_map.82.model, f32[8,4352]{1,0:T(8,128)S(1)} %select_maximum_fusion.weights), custom_call_target="tpu_custom_call" | custom-call | tf_op jit(solution)/shard_map/pallas_call | solution.py:377
  (15 shorter events, 0.3 us)
Async XLA Ops:
  0.0 1.0 copy-start
  0.0 140.1 %copy-start.2 = (bf16[1,32,256,128]{3,2,1,0:T(8,128)(2,1)S(1)}, bf16[1,32,256,128]{3,2,1,0:T(8,128)(2,1)}, u32[]{:S(2)}) copy-start(bf16[1,32,256,128]{3,2,1,0:T(8,128)(2,1)} %param.9) | copy-start | bytes 6291460
  1.2 138.9 %copy-start.1 = (f32[1,512,4096]{2,1,0:T(8,128)S(1)}, f32[1,512,4096]{2,1,0:T(8,128)}, u32[]{:S(2)}) copy-start(f32[1,512,4096]{2,1,0:T(8,128)} %param.8) | copy-start | bytes 25165828
  2.7 1.6 %copy-start.3 = (f32[512,512]{1,0:T(8,128)S(1)}, f32[512,512]{1,0:T(8,128)}, u32[]{:S(2)}) copy-start(f32[512,512]{1,0:T(8,128)} %template.1) | copy-start | bytes 3145732
  4.3 135.8 %copy-start.4 = (s32[1,32]{1,0:T(1,128)S(1)}, s32[1,32]{1,0:T(1,128)}, u32[]{:S(2)}) copy-start(s32[1,32]{1,0:T(1,128)} %param.10) | copy-start | bytes 388

commit v3 on v2

--- a/solution.py
+++ b/solution.py
@@ -1,5 +1,4 @@
 import functools
-import heapq
 
 import jax
 import jax.numpy as jnp
@@ -16,7 +15,7 @@
 HALO = 16
 EDGE = 128
 BAND = 128
-CHUNKS = 4
+CHUNKS = 2
 LINES = 128
 
 
@@ -54,45 +53,22 @@
     return best
 
 
-def routes(outer, inner, me, q, c):
-    z, x = divmod(me, inner)
-    qz, qx = divmod(q, inner)
-    detour = inner == 2 and outer > 2 and c >= CHUNKS // 2 and qz in (0, outer - 1)
-    along = qx == x or detour
-    return (
-        along and qz >= z > 0,
-        along and qz <= z < outer - 1,
-        (q == me or (not detour and qx >= x)) and x > 0,
-        (q == me or (not detour and qx <= x)) and x < inner - 1,
-    )
-
-
 def arrival_events(count):
     inner = inner_size(count)
-    outer = count // inner
-    steps = (-inner, inner, -1, 1)
-    queue, free, tick = [], {}, 0
-    seen = [[] for _ in range(count)]
-    for q in range(count):
-        for d in range(4):
-            for c in range(CHUNKS) if d < 2 else reversed(range(CHUNKS)):
-                if routes(outer, inner, q, q, c)[d]:
-                    heapq.heappush(queue, (0, tick, q, d, q, c))
-                    tick += 1
-    while queue:
-        ready, _, me, d, q, c = heapq.heappop(queue)
-        if ready < free.get((me, d), 0):
-            heapq.heappush(queue, (free[me, d], tick, me, d, q, c))
-            tick += 1
-            continue
-        free[me, d] = ready + 1
-        there = me + steps[d]
-        seen[there].append((ready + 1, tick, q * CHUNKS + c))
-        for onward in range(4):
-            if routes(outer, inner, there, q, c)[onward]:
-                heapq.heappush(queue, (ready + 1, tick, there, onward, q, c))
-                tick += 1
-    return [[event for _, _, event in sorted(arrivals)] for arrivals in seen]
+    events = []
+    for me in range(count):
+        z, x = divmod(me, inner)
+        near = sorted(range(count // inner), key=lambda other: (abs(other - z), other))
+        keys = []
+        for q in range(count):
+            if q == me:
+                continue
+            qz, qx = divmod(q, inner)
+            away = abs(qz - z)
+            time = away if qx == x else max(near.index(qz), away) + abs(qx - x)
+            keys.append((time, qx != x, q))
+        events.append([q * CHUNKS + c for _, _, q in sorted(keys) for c in range(CHUNKS)])
+    return events
 
 
 DIGIT = 256
@@ -170,8 +146,8 @@
             device_id=(row + (-1 if d == 0 else 1), me),
         )
 
-    for d in (0, 2, 1, 3):
-        for c in range(CHUNKS) if d < 2 else reversed(range(CHUNKS)):
+    for c in range(CHUNKS):
+        for d in range(4):
             @pl.when(there[d])
             def _():
                 send(me, c, d, True).start()
@@ -251,17 +227,12 @@
 
     def paths(q, c):
         qz, qx = q // inner, q % inner
-        detour = jnp.zeros((), jnp.bool_)
-        if inner == 2 and outer > 2:
-            detour = (c >= CHUNKS // 2) & ((qz == 0) | (qz == outer - 1))
-        own = q == me
-        along = (qx == x) | detour
-        level = jnp.logical_not(detour)
+        along = qx == x
         return (
             along & (qz >= z) & there[0],
             along & (qz <= z) & there[1],
-            (own | level & (qx >= x)) & there[2],
-            (own | level & (qx <= x)) & there[3],
+            (qx >= x) & there[2],
+            (qx <= x) & there[3],
         )
 
     table = arrival_codes(count)

time: 146 us -> 111 us (0.76)
  the two profiles are of different devices: /device:TPU:29 before, /device:TPU:1 now
where the time goes in v3:
time: 111 us
  Pallas kernels  106 us (95%)
  local copies, waits for them, and re-layouts  2.29 us (2%)
  other arithmetic  1.92 us (2%)
    pallas_call x1, Pallas kernels, on_device(): pl.pallas_call(functools.partial(model_kernel, count, ccd_count), out_sha...  100 us
    pallas_call x1, Pallas kernels, on_device(): pl.pallas_call(difference_kernel, grid=(rows // lines,), out_shape=jax.Sh...  5.85 us

profile of v3, /device:TPU:1, one launch (start us, length us, event | category | flops | bytes accessed | tf_op | source)
XLA Modules:
  0.0 110.5 jit_solution(4288420387409853821)
XLA Ops:
  0.0 0.0 copy-start
  0.0 0.0 copy-start.2
  0.0 0.9 fusion.2
  0.9 0.1 broadcast_bitcast_fusion.3
  1.0 0.0 copy-done
  1.0 0.1 constant_dynamic-slice_fusion.1
  1.1 0.2 copy.13
  1.2 0.0 copy-start.1
  1.2 0.1 multiply_reduce_fusion
  1.3 0.9 multiply_bitcast_fusion
  2.3 0.1 broadcast_bitcast_fusion.2
  2.4 0.1 broadcast_bitcast_fusion
  2.5 0.1 broadcast_bitcast_fusion.1
  2.7 0.0 copy-start.3
  2.7 1.6 %copy-done.3 = f32[512,512]{1,0:T(8,128)S(1)} copy-done((f32[512,512]{1,0:T(8,128)S(1)}, f32[512,512]{1,0:T(8,128)}, u32[]{:S(2)}) %copy-start.3) | copy-done | bytes 1048600
  4.3 0.0 copy-start.4
  4.3 100.3 %shard_map.82.model = f32[512,4096]{1,0:T(8,128)S(1)} custom-call(f32[512,512]{1,0:T(8,128)S(1)} %copy-done.3, f32[8,4352]{1,0:T(8,128)S(1)} %select_maximum_fusion.weights), custom_call_target="tpu_custom_call" | custom-call | tf_op jit(solution)/shard_map/pallas_call | solution.py:326
  104.6 0.0 copy-done.2
  104.7 0.0 copy-done.1
  104.7 0.0 copy-done.4
  104.7 5.8 %shard_map.83 = f32[512,4096]{1,0:T(8,128)} custom-call(s32[32]{0:T(128)S(1)} %bitcast.40, f32[512,4096]{1,0:T(8,128)S(1)} %bitcast.38, bf16[32,256,128]{2,1,0:T(8,128)(2,1)S(1)} %bitcast.39, f32[512,4096]{1,0:T(8,128)S(1)} %shard_map.82.model, f32[8,4352]{1,0:T(8,128)S(1)} %select_maximum_fusion.weights), custom_call_target="tpu_custom_call" | custom-call | tf_op jit(solution)/shard_map/pallas_call | solution.py:348
  (15 shorter events, 0.3 us)
Async XLA Ops:
  0.0 1.0 copy-start
  0.0 104.6 %copy-start.2 = (bf16[1,32,256,128]{3,2,1,0:T(8,128)(2,1)S(1)}, bf16[1,32,256,128]{3,2,1,0:T(8,128)(2,1)}, u32[]{:S(2)}) copy-start(bf16[1,32,256,128]{3,2,1,0:T(8,128)(2,1)} %param.9) | copy-start | bytes 6291460
  1.2 103.4 %copy-start.1 = (f32[1,512,4096]{2,1,0:T(8,128)S(1)}, f32[1,512,4096]{2,1,0:T(8,128)}, u32[]{:S(2)}) copy-start(f32[1,512,4096]{2,1,0:T(8,128)} %param.8) | copy-start | bytes 25165828
  2.7 1.6 %copy-start.3 = (f32[512,512]{1,0:T(8,128)S(1)}, f32[512,512]{1,0:T(8,128)}, u32[]{:S(2)}) copy-start(f32[512,512]{1,0:T(8,128)} %template.1) | copy-start | bytes 3145732
  4.3 100.4 %copy-start.4 = (s32[1,32]{1,0:T(1,128)S(1)}, s32[1,32]{1,0:T(1,128)}, u32[]{:S(2)}) copy-start(s32[1,32]{1,0:T(1,128)} %param.10) | copy-start | bytes 388

commit v4 on v3

--- a/solution.py
+++ b/solution.py
@@ -15,7 +15,7 @@
 HALO = 16
 EDGE = 128
 BAND = 128
-CHUNKS = 2
+CHUNKS = 4
 LINES = 128
 
 

time: 111 us -> 112 us (level)
    pallas_call x1, Pallas kernels: 100 us -> 102 us  [on_device(): pl.pallas_call(functools.partial(model_kernel, count, ccd_count), out_sha...]
where the time goes in v4:
time: 112 us
  Pallas kernels  107 us (96%)
  local copies, waits for them, and re-layouts  2.29 us (2%)
  other arithmetic  1.92 us (2%)
    pallas_call x1, Pallas kernels, on_device(): pl.pallas_call(functools.partial(model_kernel, count, ccd_count), out_sha...  102 us
    pallas_call x1, Pallas kernels, on_device(): pl.pallas_call(difference_kernel, grid=(rows // lines,), out_shape=jax.Sh...  5.88 us

profile of v4, /device:TPU:1, one launch (start us, length us, event | category | flops | bytes accessed | tf_op | source)
XLA Modules:
  0.0 111.8 jit_solution(11929464119792541868)
XLA Ops:
  0.0 0.0 copy-start
  0.0 0.0 copy-start.2
  0.0 0.9 fusion.2
  0.9 0.1 broadcast_bitcast_fusion.3
  1.0 0.0 copy-done
  1.0 0.1 constant_dynamic-slice_fusion.1
  1.1 0.2 copy.13
  1.2 0.0 copy-start.1
  1.2 0.1 multiply_reduce_fusion
  1.3 0.9 multiply_bitcast_fusion
  2.3 0.1 broadcast_bitcast_fusion.2
  2.4 0.1 broadcast_bitcast_fusion
  2.5 0.1 broadcast_bitcast_fusion.1
  2.7 0.0 copy-start.3
  2.7 1.6 %copy-done.3 = f32[512,512]{1,0:T(8,128)S(1)} copy-done((f32[512,512]{1,0:T(8,128)S(1)}, f32[512,512]{1,0:T(8,128)}, u32[]{:S(2)}) %copy-start.3) | copy-done | bytes 1048600
  4.3 0.0 copy-start.4
  4.3 101.6 %shard_map.82.model = f32[512,4096]{1,0:T(8,128)S(1)} custom-call(f32[512,512]{1,0:T(8,128)S(1)} %copy-done.3, f32[8,4352]{1,0:T(8,128)S(1)} %select_maximum_fusion.weights), custom_call_target="tpu_custom_call" | custom-call | tf_op jit(solution)/shard_map/pallas_call | solution.py:326
  105.9 0.0 copy-done.2
  105.9 0.0 copy-done.1
  105.9 0.0 copy-done.4
  105.9 5.9 %shard_map.83 = f32[512,4096]{1,0:T(8,128)} custom-call(s32[32]{0:T(128)S(1)} %bitcast.40, f32[512,4096]{1,0:T(8,128)S(1)} %bitcast.38, bf16[32,256,128]{2,1,0:T(8,128)(2,1)S(1)} %bitcast.39, f32[512,4096]{1,0:T(8,128)S(1)} %shard_map.82.model, f32[8,4352]{1,0:T(8,128)S(1)} %select_maximum_fusion.weights), custom_call_target="tpu_custom_call" | custom-call | tf_op jit(solution)/shard_map/pallas_call | solution.py:348
  (15 shorter events, 0.3 us)
Async XLA Ops:
  0.0 1.0 copy-start
  0.0 105.9 %copy-start.2 = (bf16[1,32,256,128]{3,2,1,0:T(8,128)(2,1)S(1)}, bf16[1,32,256,128]{3,2,1,0:T(8,128)(2,1)}, u32[]{:S(2)}) copy-start(bf16[1,32,256,128]{3,2,1,0:T(8,128)(2,1)} %param.9) | copy-start | bytes 6291460
  1.2 104.7 %copy-start.1 = (f32[1,512,4096]{2,1,0:T(8,128)S(1)}, f32[1,512,4096]{2,1,0:T(8,128)}, u32[]{:S(2)}) copy-start(f32[1,512,4096]{2,1,0:T(8,128)} %param.8) | copy-start | bytes 25165828
  2.7 1.6 %copy-start.3 = (f32[512,512]{1,0:T(8,128)S(1)}, f32[512,512]{1,0:T(8,128)}, u32[]{:S(2)}) copy-start(f32[512,512]{1,0:T(8,128)} %template.1) | copy-start | bytes 3145732
  4.3 101.6 %copy-start.4 = (s32[1,32]{1,0:T(1,128)S(1)}, s32[1,32]{1,0:T(1,128)}, u32[]{:S(2)}) copy-start(s32[1,32]{1,0:T(1,128)} %param.10) | copy-start | bytes 388
